TPU v7x, 32 devices: a whole 2x2x4 slice. The times are simulated.
32 devices in a mesh: groups: 2 (over y), dp: 8 (over z, x), tensor: 2 (over core).
Axes of the slice: x: 2, y: 2, z: 4, core: 2. Of those that a mesh axis runs over, the one named last changes fastest.
Arguments:
- tokens: bfloat16 [2048, 8192], P(('groups', 'dp'), 'tensor'), parts along dimension 0, may hold values from -4 to 4
- gate_weight_base: bfloat16 [14336, 8192], P('dp', 'tensor'), may hold values from -0.0625 to 0.0625
- up_weight_base: bfloat16 [14336, 8192], P('dp', 'tensor'), may hold values from -0.0625 to 0.0625
- adapter_down_stack: bfloat16 [8, 8192, 128], P('dp', 'tensor'), may hold values from -0.0625 to 0.0625
- adapter_up_stack: bfloat16 [8, 128, 14336], P('dp', 'tensor'), may hold values from -2 to 2
- segment_block_counts: int32 [8], P('groups'), parts along dimension 0, may hold values from 1 to 3, 8 in all
- segment_adapter_ids: int32 [8], P('groups'), parts along dimension 0, may hold values from 0 to 7
- segment_live_rows: int32 [8], P('groups'), parts along dimension 0, may hold values from 1 to 128
Outputs:
- ref_hidden: bfloat16 [14336, 2048], P('dp', ('groups', 'tensor')), parts along dimension 1
- pol_hidden: bfloat16 [14336, 2048], P('dp', ('groups', 'tensor')), parts along dimension 1
- seg_kl: float32 [8], P('groups'), parts along dimension 0
There are 2 independent parts, one for each index of `groups`. A program takes and returns all parts, laid end to end along the dimension named above; an argument that names none is the same for every part. Nothing has to cross between parts.
All inputs are finite; a program needn't handle non-finite values.
Results may differ from a plain program's by a relative error of at most 0.0052.
Values may be sent and summed in bfloat16 or wider, within the bound.
A program may use at most 192 MiB of HBM per device.

v0:
```python
import jax
import jax.numpy as jnp
from jax import lax
from jax.sharding import PartitionSpec as P

BLOCK = 128


def spread_2(value, axis, root):
    mine = lax.axis_index(axis) == root
    return lax.psum(jnp.where(mine, value, jnp.zeros_like(value)), axis)


def segment_tables(segment_block_counts, segment_live_rows, total_rows):
    seg_ends = jnp.cumsum(segment_block_counts)
    starts = seg_ends - segment_block_counts
    row_ids = jnp.arange(total_rows, dtype=jnp.int32)
    blocks = row_ids // BLOCK
    member = (blocks[None, :] >= starts[:, None]) & (blocks[None, :] < seg_ends[:, None])
    live_limit = (seg_ends - 1) * BLOCK + segment_live_rows
    live_rows = member & (row_ids[None, :] < live_limit[:, None])
    counts = (live_limit - starts * BLOCK).astype(jnp.float32)
    return (member, live_rows, counts)


def project_tokens(tokens, gate_weight_base, up_weight_base, adapter_down_matrix, owned_rows):
    contract = (((1,), (1,)), ((), ()))
    rank_pair = adapter_down_matrix.shape[1]
    block_rows = lax.all_gather(tokens, "dp", axis=0, tiled=True)
    row_count = block_rows.shape[0]
    gate_part = lax.dot_general(
        gate_weight_base, block_rows, contract, preferred_element_type=jnp.float32
    )
    up_part = lax.dot_general(
        up_weight_base, block_rows, contract, preferred_element_type=jnp.float32
    )
    base_terms = jnp.stack([gate_part, up_part])
    contrib = lax.cond(
        jnp.any(owned_rows),
        lambda: jnp.dot(block_rows, adapter_down_matrix, preferred_element_type=jnp.float32)
        * owned_rows[:, None].astype(jnp.float32),
        lambda: jnp.zeros((row_count, rank_pair), jnp.float32),
    )
    return (base_terms, contrib)


def shards(
    tokens,
    gate_weight_base,
    up_weight_base,
    adapter_down_stack,
    adapter_up_stack,
    segment_block_counts,
    segment_adapter_ids,
    segment_live_rows,
):
    dp_count = lax.axis_size("dp")
    tp_count = lax.axis_size("tensor")
    dp_index = lax.axis_index("dp")
    tp_index = lax.axis_index("tensor")
    local_rows = tokens.shape[0]
    total_rows = local_rows * dp_count
    rows_half = total_rows // tp_count
    seg_count = segment_block_counts.shape[0]
    member, live_rows, counts = segment_tables(segment_block_counts, segment_live_rows, total_rows)
    adapter_down_matrix = adapter_down_stack[0]
    rank_pair = adapter_down_matrix.shape[1]
    base_terms, unused_terms = project_tokens(
        tokens,
        gate_weight_base,
        up_weight_base,
        adapter_down_matrix,
        jnp.zeros((total_rows,), jnp.bool_),
    )
    home_first = dp_index * local_rows
    home_member = lax.dynamic_slice_in_dim(member, home_first, local_rows, 1).astype(jnp.float32)

    def fetch_slot(buffer_slot, accum):
        fetched = spread_2(adapter_down_matrix, "dp", segment_adapter_ids[buffer_slot])
        return (
            accum
            + jnp.dot(tokens, fetched, preferred_element_type=jnp.float32)
            * home_member[buffer_slot][:, None]
        )

    home_terms = lax.fori_loop(
        0, seg_count, fetch_slot, jnp.zeros((local_rows, rank_pair), jnp.float32)
    )
    down_terms = lax.dynamic_update_slice_in_dim(
        jnp.zeros((total_rows, rank_pair), jnp.float32), home_terms, home_first, 0
    )
    down_proj = lax.psum(down_terms, ("dp", "tensor")).astype(jnp.bfloat16)
    slice_list = lax.all_to_all(adapter_up_stack, "dp", split_axis=2, concat_axis=0, tiled=True)
    adapters = slice_list.shape[0]
    rank_part = slice_list.shape[1]
    ff_dev = slice_list.shape[2]
    picker = (
        segment_adapter_ids[:, None] == jnp.arange(adapters, dtype=jnp.int32)[None, :]
    ).astype(jnp.bfloat16)
    chosen = jnp.einsum(
        "sa,aqf->sqf", picker, slice_list, preferred_element_type=jnp.float32
    ).astype(jnp.bfloat16)
    own_ranks = lax.dynamic_slice_in_dim(down_proj, tp_index * rank_part, rank_part, 1)
    spread = (member.T.astype(jnp.bfloat16)[:, :, None] * own_ranks[:, None, :]).reshape(
        total_rows, seg_count * rank_part
    )
    delta_cols = lax.dot_general(
        chosen.reshape(seg_count * rank_part, ff_dev),
        spread,
        (((0,), (1,)), ((), ())),
        preferred_element_type=jnp.float32,
    )
    upper = tp_index >= tp_count // 2
    blank = jnp.zeros_like(delta_cols)
    policy_terms = base_terms + jnp.stack(
        [jnp.where(upper, blank, delta_cols), jnp.where(upper, delta_cols, blank)]
    )
    halves = lax.psum_scatter(
        jnp.stack([base_terms, policy_terms]), "tensor", scatter_dimension=3, tiled=True
    )
    ref_hidden = (jax.nn.silu(halves[0, 0]) * halves[0, 1]).astype(jnp.bfloat16)
    pol_hidden = (jax.nn.silu(halves[1, 0]) * halves[1, 1]).astype(jnp.bfloat16)
    ref_vals = 4.0 * jnp.tanh(ref_hidden.astype(jnp.float32) * 0.25)
    pol_vals = 4.0 * jnp.tanh(pol_hidden.astype(jnp.float32) * 0.25)
    pol_exp = jnp.exp(pol_vals)
    first_half = tp_index * rows_half

    def placed(values):
        return lax.dynamic_update_slice_in_dim(
            jnp.zeros((total_rows,), jnp.float32), values, first_half, 0
        )

    ref_sum, pol_sum, cross_sum = lax.psum(
        (
            placed(jnp.sum(jnp.exp(ref_vals), axis=0)),
            placed(jnp.sum(pol_exp, axis=0)),
            placed(jnp.sum(pol_exp * (pol_vals - ref_vals), axis=0)),
        ),
        ("dp", "tensor"),
    )
    kl_row = cross_sum / pol_sum - jnp.log(pol_sum) + jnp.log(ref_sum)
    seg_kl = jnp.sum(live_rows.astype(jnp.float32) * kl_row[None, :], axis=1) / counts
    return (ref_hidden, pol_hidden, seg_kl)


def solution(mesh):
    in_specs = (
        P(("groups", "dp"), "tensor"),
        P("dp", "tensor"),
        P("dp", "tensor"),
        P("dp", "tensor", None),
        P("dp", "tensor", None),
        P("groups"),
        P("groups"),
        P("groups"),
    )
    out_specs = (P("dp", ("groups", "tensor")), P("dp", ("groups", "tensor")), P("groups"))
    return jax.shard_map(shards, mesh=mesh, in_specs=in_specs, out_specs=out_specs, check_vma=False)
```

profile of v0, /device:TPU:0, one launch (start us, length us, event | category | flops | bytes accessed | tf_op | source)
XLA Modules:
  0.0 786.8 jit_solution(14287814652710605541)
XLA Ops:
  9.6 341.4 %while.14 = (s32[]{:T(128)}, f32[128,128]{0,1:T(8,128)S(1)}, s32[4]{0:T(128)}, bf16[4096,128]{1,0:T(8,128)(2,1)}, bf16[128,4096]{1,0:T(8,128)(2,1)}, /*index=5*/...) while((s32[]{:T(128)}, f32[128,128]{0,1:T(8,128)S(1)}, s32[4]{0:T(128)}, ...), condition=%wide.region_3.4_spmd.clone, body=%wide.region_1.3_spmd.clone.sunk | while | flops 135315456 | bytes 10618585 | solution.py:86
  9.7 1.4 dynamic_slice.31
  11.7 1.1 broadcast_select_fusion.2
  12.8 82.5 %all-reduce.4.cloned.1.call-done = bf16[4096,128]{1,0:T(8,128)(2,1)} async-done(((bf16[4096,128]{1,0:T(8,128)(2,1)}), bf16[4096,128]{1,0:T(8,128)(2,1)}) %all-reduce.4.cloned.1.call-update) | async-done | bytes 1048592 | tf_op jit(solution)/shard_map/while/body/eval_jaxpr/psum | solution.py:11
  95.3 2.0 fusion.41
  97.4 1.2 dynamic_slice.31
  99.3 2.3 broadcast_select_fusion.2
  101.6 78.3 %all-reduce.4.cloned.1.call-done = bf16[4096,128]{1,0:T(8,128)(2,1)} async-done(((bf16[4096,128]{1,0:T(8,128)(2,1)}), bf16[4096,128]{1,0:T(8,128)(2,1)}) %all-reduce.4.cloned.1.call-update) | async-done | bytes 1048592 | tf_op jit(solution)/shard_map/while/body/eval_jaxpr/psum | solution.py:11
  179.9 2.0 fusion.41
  182.0 1.2 dynamic_slice.31
  185.0 79.6 %all-reduce.4.cloned.1.call-done = bf16[4096,128]{1,0:T(8,128)(2,1)} async-done(((bf16[4096,128]{1,0:T(8,128)(2,1)}), bf16[4096,128]{1,0:T(8,128)(2,1)}) %all-reduce.4.cloned.1.call-update) | async-done | bytes 1048592 | tf_op jit(solution)/shard_map/while/body/eval_jaxpr/psum | solution.py:11
  264.6 2.0 fusion.41
  266.7 1.2 dynamic_slice.31
  269.7 79.3 %all-reduce.4.cloned.1.call-done = bf16[4096,128]{1,0:T(8,128)(2,1)} async-done(((bf16[4096,128]{1,0:T(8,128)(2,1)}), bf16[4096,128]{1,0:T(8,128)(2,1)}) %all-reduce.4.cloned.1.call-update) | async-done | bytes 1048592 | tf_op jit(solution)/shard_map/while/body/eval_jaxpr/psum | solution.py:11
  349.0 2.0 fusion.41
  351.6 11.6 %copy.12 = bf16[1,64,14336]{1,0,2:T(2,128)(2,1)} copy(bf16[1,64,14336]{2,1,0:T(8,128)(2,1)S(1)} %copy-done.1) | data formatting | bytes 3670016 | tf_op args[4]
  363.8 79.7 %reduce = bf16[14336,64]{1,0:T(8,128)(2,1)} reduce(bf16[14336,1,64]{2,1,0:T(2,128)(2,1)} %bitcast.91, bf16[]{:T(256)} %broadcast.130), dimensions={1}, to_apply=%bitcast.63.reduce_sub_computation | reduce | bytes 3670018
  443.5 7.2 reshape.166
  450.7 4.2 all-to-all-start
  455.1 109.3 %all-reduce.5 = bf16[1024,128]{0,1:T(8,128)(2,1)S(1)} all-reduce(f32[1024,128]{0,1:T(8,128)S(1)} %constant_dynamic-update-slice_fusion), channel_id=1, replica_groups=mesh['groups'=2,'dp'=8,'tensor'=2] {'dp','tensor'}, use_global_device_ids=true, to_apply=%region_4.5 | all-reduce | flops 131072 | bytes 786432 | tf_op jit(solution)/shard_map/psum | solution.py:92
  564.5 5.5 reshape.167
  570.0 14.0 %copy.13 = bf16[1,64,14336]{2,1,0:T(8,128)(2,1)S(1)} copy(bf16[1,64,14336]{1,0,2:T(2,128)(2,1)} %bitcast.92) | data formatting | bytes 3670016 | tf_op jit(solution)/shard_map/all_to_all | solution.py:93
  585.1 6.4 fusion.2
  591.5 21.9 %fusion.28 = f32[1792,1024]{1,0:T(8,128)} fusion(bf16[1792,4096]{1,0:T(8,128)(2,1)} %param.11, bf16[1024,4096]{1,0:T(8,128)(2,1)} %all-gather.2.cloned.1.call-done), kind=kOutput, calls=%fused_computation.55 | convolution fusion | flops 15032385536 | bytes 30408704 | tf_op jit(solution)/shard_map/dot_general | solution.py:31
  613.4 19.4 %fusion.29 = f32[1792,1024]{1,0:T(8,128)} fusion(bf16[1792,4096]{1,0:T(8,128)(2,1)} %param.12, bf16[1024,4096]{1,0:T(8,128)(2,1)S(1)} %copy-done.3), kind=kOutput, calls=%fused_computation.56 | convolution fusion | flops 15032385536 | bytes 30408704 | tf_op jit(solution)/shard_map/dot_general | solution.py:34
  632.7 13.7 %maximum_bitcast_fusion = f32[1,2,1792,1024]{3,2,1,0:T(8,128)} fusion(f32[1,1792,1024]{2,1,0:T(8,128)} %bitcast.89, f32[1,1792,1024]{2,1,0:T(8,128)} %bitcast.87), kind=kLoop, calls=%fused_computation.6 | loop fusion | flops 3670016 | bytes 29360128 | tf_op jit(solution)/shard_map/stack | solution.py:119
  646.4 10.7 %maximum_add_fusion = f32[1,2,1792,1024]{3,2,1,0:T(8,128)S(1)} fusion(f32[1,1,1792,1024]{3,2,1,0:T(8,128)} %bitcast.90, f32[1,1,1792,1024]{3,2,1,0:T(8,128)} %bitcast.88, f32[1,1,1792,1024]{3,2,1,0:T(8,128)} %get-tuple-element.155, f32[1,1,1792,1024]{3,2,1,0:T(8,128)} %get-tuple-element.154), kind=kLoop, calls=%fused_computation.7 | loop fusion | flops 11010048 | bytes 44040192 | tf_op jit(solution)/shard_map/add | solution.py:115
  657.1 2.9 copy-done
  660.0 10.4 %pad_maximum_fusion = f32[2,2,1792,1024]{3,2,1,0:T(8,128)} fusion(f32[1,2,1792,1024]{3,2,1,0:T(8,128)S(1)} %maximum_add_fusion, f32[1,2,1792,1024]{3,2,1,0:T(8,128)S(1)} %copy-done), kind=kLoop, calls=%fused_computation.5 | loop fusion | flops 7340032 | bytes 58720256 | tf_op jit(solution)/shard_map/stack | solution.py:119
  670.4 37.5 %reduce-scatter.2.cloned.1.call-done = f32[2,2,1792,512]{3,2,1,0:T(8,128)} async-done(((f32[2,2,1792,1024]{3,2,1,0:T(8,128)}), f32[2,2,1792,512]{3,2,1,0:T(8,128)}) %reduce-scatter.2.cloned.1.call-update) | async-done | bytes 14680080 | tf_op jit(solution)/shard_map/reduce_scatter | solution.py:118
  707.8 8.5 %multiply_reduce_fusion = (f32[512]{0:T(512)S(1)}, f32[512]{0:T(512)S(1)}, f32[512]{0:T(512)S(1)}, bf16[1792,512]{1,0:T(8,128)(2,1)}, bf16[1792,512]{1,0:T(8,128)(2,1)}) fusion(f32[2,2,1792,512]{3,2,1,0:T(8,128)} %reduce-scatter.2.cloned.1.call-done), kind=kLoop, calls=%fused_computation.21 | loop fusion | flops 21101056 | bytes 18356224 | tf_op jit(solution)/shard_map/reduce_sum | solution.py:137
  717.0 61.9 %all-reduce = (f32[1024]{0:T(1024)S(1)}, f32[1024]{0:T(1024)S(1)}, f32[1024]{0:T(1024)S(1)}) all-reduce(f32[1024]{0:T(1024)S(1)} %dynamic_update_slice.15, f32[1024]{0:T(1024)S(1)} %dynamic_update_slice.14, f32[1024]{0:T(1024)S(1)} %dynamic_update_slice.13), channel_id=1, replica_groups=mesh['groups'=2,'dp'=8,'tensor'=2] {'dp','tensor'}, use_global_device_ids=true, to_apply=%region_11.12 | all-reduce | flops 3072 | bytes 24576 | tf_op jit(solution)/shard_map/psum | solution.py:133
  (49 shorter events, 7.7 us)
Async XLA Ops:
  9.6 342.0 %copy-start.1 = (bf16[1,64,14336]{2,1,0:T(8,128)(2,1)S(1)}, bf16[1,64,14336]{2,1,0:T(8,128)(2,1)}, u32[]{:S(2)}) copy-start(bf16[1,64,14336]{2,1,0:T(8,128)(2,1)} %param.14) | copy-start | bytes 5505028
  9.6 85.6 %all-reduce.4.cloned.1.call-start = ((), (), s32[]{:S(2)}) async-start(), calls=%async_computation.4 | async-start | bytes 2097152 | tf_op jit(solution)/shard_map/while/body/eval_jaxpr/psum | solution.py:11
  97.3 82.6 %all-reduce.4.cloned.1.call-start = ((), (), s32[]{:S(2)}) async-start(), calls=%async_computation.4 | async-start | bytes 2097152 | tf_op jit(solution)/shard_map/while/body/eval_jaxpr/psum | solution.py:11
  182.0 82.7 %all-reduce.4.cloned.1.call-start = ((), (), s32[]{:S(2)}) async-start(), calls=%async_computation.4 | async-start | bytes 2097152 | tf_op jit(solution)/shard_map/while/body/eval_jaxpr/psum | solution.py:11
  266.7 82.3 %all-reduce.4.cloned.1.call-start = ((), (), s32[]{:S(2)}) async-start(), calls=%async_computation.4 | async-start | bytes 2097152 | tf_op jit(solution)/shard_map/while/body/eval_jaxpr/psum | solution.py:11
  351.1 240.4 %all-gather.2.cloned.1.call-start = ((), (), s32[]{:S(2)}) async-start(), calls=%async_computation.2 | async-start | bytes 9437184 | tf_op jit(solution)/shard_map/all_gather | solution.py:29
  450.7 113.8 %all-to-all-start = ((bf16[8,2,57344]{2,1,0:T(2,128)(2,1)}), bf16[8,2,57344]{2,1,0:T(2,128)(2,1)S(1)}, u32[]{:S(2)}, u32[]{:S(2)}) async-start(bf16[8,2,57344]{2,1,0:T(2,128)(2,1)} %reshape.166), calls=%async_computation | async-start | bytes 3670016 | tf_op jit(solution)/shard_map/all_to_all | solution.py:93
  454.9 252.9 %reduce-scatter.2.cloned.1.call-start = ((), (), s32[]{:S(2)}) async-start(), calls=%async_computation.3 | async-start | bytes 44040192 | tf_op jit(solution)/shard_map/reduce_scatter | solution.py:118
  570.0 14.4 %copy-start.2 = (s32[4]{0:T(128)S(1)}, s32[4]{0:T(128)}, u32[]{:S(2)}) copy-start(s32[4]{0:T(128)} %get-tuple-element.240) | copy-start | bytes 52
  591.5 21.9 %copy-start.3 = (bf16[1024,4096]{1,0:T(8,128)(2,1)S(1)}, bf16[1024,4096]{1,0:T(8,128)(2,1)}, u32[]{:S(2)}) copy-start(bf16[1024,4096]{1,0:T(8,128)(2,1)} %all-gather.2.cloned.1.call-done) | copy-start | bytes 25165828
  646.4 13.6 %copy-start = (f32[1,2,1792,1024]{3,2,1,0:T(8,128)S(1)}, f32[1,2,1792,1024]{3,2,1,0:T(8,128)}, u32[]{:S(2)}) copy-start(f32[1,2,1792,1024]{3,2,1,0:T(8,128)} %maximum_bitcast_fusion) | copy-start | bytes 44040196
Sparse Core Ops, SparseCore 0:
  14.6 80.6 all-reduce.3
  102.3 77.6 all-reduce.3
  186.9 77.6 all-reduce.3
  271.3 77.6 all-reduce.3
Sparse Core Ops, SparseCore 1:
  353.7 144.5 all-gather.1
  670.5 37.3 reduce-scatter.1
where the time goes:
time: 788 us; the launch traced here: 787 us
  waiting for transfers between devices  358 us (45%)
  blocking collectives  171 us (22%)
  other arithmetic  131 us (17%)
  matrix products  56.4 us (7%)
  local copies, waits for them, and re-layouts  48 us (6%)
  between operations  15.3 us (2%)
    psum x4, waiting for transfers between devices, spread_2(): return lax.psum(jnp.where(mine, value, jnp.zeros_like(value)), axis)  320 us
    psum x1, blocking collectives, shards(): down_proj = lax.psum(down_terms, ('dp', 'tensor')).astype(jnp.bfloat16)  109 us
    unnamed x2, other arithmetic  79.7 us
    psum x1, blocking collectives, shards(): lax.psum((placed(jnp.sum(jnp.exp(ref_vals), axis=0)), placed(jnp.sum(pol_...  61.9 us
    reduce_scatter x1, waiting for transfers between devices, shards(): lax.psum_scatter(jnp.stack([base_terms, policy_terms]), 'tensor', scatter...  37.5 us
    unnamed x13, local copies, waits for them, and re-layouts  28.2 us
    another operation x2, other arithmetic, shards(): jnp.stack([base_terms, policy_terms])  24 us
    dot_general x1, matrix products, project_tokens(): lax.dot_general(gate_weight_base, block_rows, contract, preferred_element...  21.9 us
  transfers between devices with their start and end apart: 7, of which 5 were waited for; matrix products, arithmetic and copies ran while one was open for 16% of the time, Pallas kernels for 0%

commit v1 on v0

--- a/solution.py
+++ b/solution.py
@@ -1,6 +1,9 @@
+import functools
 import jax
 import jax.numpy as jnp
 from jax import lax
+from jax.experimental import pallas as pl
+from jax.experimental.pallas import tpu as pltpu
 from jax.sharding import PartitionSpec as P
 
 BLOCK = 128
@@ -143,6 +146,329 @@
     return (ref_hidden, pol_hidden, seg_kl)
 
 
+MESH = pl.DeviceIdType.MESH
+
+
+def ring_place(dp_index, count):
+    odd = dp_index % 2
+    return odd * (count - 1 - dp_index // 2) + (1 - odd) * (dp_index // 2)
+
+
+def ring_index(place, count):
+    upper = place // (count // 2)
+    return (1 - upper) * 2 * place + upper * (2 * (count - 1 - place) + 1)
+
+
+def gather_project(
+    dp_count, tp_count, group_count, unit_chunk,
+    tokens, gate, up, down, adapter_up,
+    own_out, peer_out, adapters_out, contrib_out,
+    tok_buf, weights, down_buf, parts, contrib,
+    load_sem, ring_send, ring_recv, ad_send, ad_recv, pass_send, pass_recv,
+    part_send, part_recv, out_sem,
+):
+    half = dp_count // 2
+    rows = tokens.shape[0]
+    units = gate.shape[0]
+    ranks = adapter_up.shape[0]
+    me = lax.axis_index("dp")
+    core = lax.axis_index("tensor")
+    group = lax.axis_index("groups")
+    place = ring_place(me, dp_count)
+    right = ring_index((place + 1) % dp_count, dp_count)
+    left = ring_index((place + dp_count - 1) % dp_count, dp_count)
+    other_core = 1 - core
+    other_group = 1 - group
+
+    barrier = pltpu.get_barrier_semaphore()
+    for k in range(1, dp_count):
+        pl.semaphore_signal(barrier, inc=1, device_id={"dp": (me + k) % dp_count}, device_id_type=MESH)
+    pl.semaphore_signal(barrier, inc=1, device_id={"tensor": other_core}, device_id_type=MESH)
+    pl.semaphore_signal(barrier, inc=1, device_id={"groups": other_group}, device_id_type=MESH)
+    pl.semaphore_wait(barrier, dp_count + 1)
+
+    def block(slot):
+        return tok_buf.at[pl.ds(slot * rows, rows)]
+
+    def send(src, dst, sem, axis, target, sends, recvs):
+        copy = pltpu.make_async_remote_copy(
+            src_ref=src, dst_ref=dst, send_sem=sends.at[sem], recv_sem=recvs.at[sem],
+            device_id={axis: target}, device_id_type=MESH,
+        )
+        copy.start()
+        return copy
+
+    last = dp_count - 1
+    cut = rows // 2
+    cw = send(tokens, block(1), 0, "dp", right, ring_send, ring_recv)
+    ccw = send(tokens, block(2), 1, "dp", left, ring_send, ring_recv)
+
+    loads = [
+        pltpu.make_async_copy(tokens, block(0), load_sem.at[0]),
+        pltpu.make_async_copy(gate, weights.at[0], load_sem.at[1]),
+        pltpu.make_async_copy(up, weights.at[1], load_sem.at[2]),
+        pltpu.make_async_copy(down, down_buf, load_sem.at[3]),
+    ]
+    for load in loads:
+        load.start()
+
+    share = ranks // group_count
+    mine = pl.ds(pl.multiple_of(group * share, 16), share)
+    landing = pl.ds(pl.multiple_of(core * ranks + group * share, 16), share)
+    ad_copies = []
+    for k in range(1, dp_count):
+        target = (me + k) % dp_count
+        ad_copies.append(send(
+            adapter_up.at[mine, pl.ds(pl.multiple_of(target * units, 128), units)],
+            adapters_out.at[me, landing], k, "dp", target, ad_send, ad_recv,
+        ))
+    ad_local = pltpu.make_async_copy(
+        adapter_up.at[mine, pl.ds(pl.multiple_of(me * units, 128), units)],
+        adapters_out.at[me, landing], load_sem.at[4],
+    )
+    ad_local.start()
+    for load in loads:
+        load.wait()
+
+    def project(slot, blocks):
+        def chunk(step, carry):
+            which = step // (units // unit_chunk)
+            first = pl.multiple_of((step % (units // unit_chunk)) * unit_chunk, unit_chunk)
+            value = lax.dot_general(
+                weights[which, pl.ds(first, unit_chunk), :],
+                tok_buf[pl.ds(slot * rows, blocks * rows), :],
+                (((1,), (1,)), ((), ())), preferred_element_type=jnp.float32,
+            )
+            for b in range(blocks):
+                parts[slot + b, which, pl.ds(first, unit_chunk), :] = value[:, b * rows:(b + 1) * rows]
+            return carry
+
+        contrib[pl.ds(slot * rows, blocks * rows), :] = jnp.dot(
+            tok_buf[pl.ds(slot * rows, blocks * rows), :], down_buf[...],
+            preferred_element_type=jnp.float32,
+        )
+        lax.fori_loop(0, 2 * (units // unit_chunk), chunk, 0)
+
+    per_core = dp_count // tp_count
+    slot_place = [place]
+    for s in range(1, half):
+        slot_place += [(place + dp_count - s) % dp_count, (place + s) % dp_count]
+    slot_place.append((place + half) % dp_count)
+    slot_block = [ring_index(q, dp_count) for q in slot_place]
+
+    def part_copy(slot):
+        where = slot_block[slot] % per_core
+        return pltpu.make_async_remote_copy(
+            src_ref=parts.at[slot], dst_ref=peer_out.at[where],
+            send_sem=part_send.at[slot], recv_sem=part_recv.at[where],
+            device_id={"tensor": other_core}, device_id_type=MESH,
+        )
+
+    def own_copy(slot):
+        where = slot_block[slot] % per_core
+        return pltpu.make_async_copy(parts.at[slot], own_out.at[where], part_send.at[slot])
+
+    def contrib_copy(slot):
+        first = pl.multiple_of(slot_block[slot] * rows, rows)
+        return pltpu.make_async_copy(
+            contrib.at[pl.ds(slot * rows, rows)], contrib_out.at[pl.ds(first, rows)], out_sem.at[slot]
+        )
+
+    def hand_over(slot):
+        contrib_copy(slot).start()
+
+        @pl.when(slot_block[slot] // per_core == core)
+        def _():
+            own_copy(slot).start()
+
+        @pl.when(slot_block[slot] // per_core != core)
+        def _():
+            part_copy(slot).start()
+
+    project(0, 1)
+    hand_over(0)
+    sent = [cw, ccw]
+    passes = []
+    for s in range(1, half):
+        cw.wait_recv()
+        ccw.wait_recv()
+        if s < half - 1:
+            cw = send(block(2 * s - 1), block(2 * s + 1), 2 * s, "dp", right, ring_send, ring_recv)
+            ccw = send(block(2 * s), block(2 * s + 2), 2 * s + 1, "dp", left, ring_send, ring_recv)
+        else:
+            a, b = (2 * s - 1) * rows, 2 * s * rows + cut
+            z = last * rows
+            cw = send(tok_buf.at[pl.ds(a, cut)], tok_buf.at[pl.ds(z, cut)],
+                      2 * s, "dp", right, ring_send, ring_recv)
+            ccw = send(tok_buf.at[pl.ds(b, cut)], tok_buf.at[pl.ds(z + cut, cut)],
+                       2 * s + 1, "dp", left, ring_send, ring_recv)
+        sent += [cw, ccw]
+        project(2 * s - 1, 2)
+        hand_over(2 * s - 1)
+        hand_over(2 * s)
+        if s == half - 2:
+            for copy in ad_copies:
+                copy.wait_recv()
+            ad_local.wait()
+            region = adapters_out.at[:, landing]
+            passes.append(send(region, region, 0, "groups", other_group, pass_send, pass_recv))
+        if s == half - 1:
+            passes[0].wait_recv()
+            region = adapters_out.at[:, pl.ds(pl.multiple_of(core * ranks, 16), ranks)]
+            passes.append(send(region, region, 1, "tensor", other_core, pass_send, pass_recv))
+    cw.wait_recv()
+    ccw.wait_recv()
+    project(last, 1)
+    hand_over(last)
+
+    for copy in sent + ad_copies + passes:
+        copy.wait_send()
+    passes[1].wait_recv()
+    for slot in range(dp_count):
+        contrib_copy(slot).wait()
+
+        @pl.when(slot_block[slot] // per_core == core)
+        def _():
+            own_copy(slot).wait()
+
+        @pl.when(slot_block[slot] // per_core != core)
+        def _():
+            part_copy(slot).wait_send()
+
+    for where in range(per_core):
+        pltpu.make_async_remote_copy(
+            src_ref=parts.at[where], dst_ref=peer_out.at[where],
+            send_sem=part_send.at[where], recv_sem=part_recv.at[where],
+            device_id={"tensor": other_core}, device_id_type=MESH,
+        ).wait_recv()
+
+
+def finish(ids, own, peer, adapters, down_proj, ref_out, pol_out, sums):
+    blocks = own.shape[0]
+    rows = own.shape[3]
+    ranks = down_proj.shape[1] // 2
+
+    @pl.when(pl.program_id(0) == 0)
+    def _():
+        sums[...] = jnp.zeros_like(sums)
+
+    def silu(v):
+        return v / (1.0 + jnp.exp(-v))
+
+    contract = (((0,), (1,)), ((), ()))
+    for j in range(blocks):
+        columns = slice(j * rows, (j + 1) * rows)
+        gate = own[j, 0] + peer[j, 0]
+        up = own[j, 1] + peer[j, 1]
+        chosen = adapters[ids[j]]
+        ref_hidden = (silu(gate) * up).astype(jnp.bfloat16)
+        ref_out[:, columns] = ref_hidden
+        gate = gate + lax.dot_general(
+            chosen[:ranks], down_proj[columns, :ranks], contract, preferred_element_type=jnp.float32
+        )
+        up = up + lax.dot_general(
+            chosen[ranks:], down_proj[columns, ranks:], contract, preferred_element_type=jnp.float32
+        )
+        pol_hidden = (silu(gate) * up).astype(jnp.bfloat16)
+        pol_out[:, columns] = pol_hidden
+        ref_vals = 4.0 * jnp.tanh(ref_hidden.astype(jnp.float32) * 0.25)
+        pol_vals = 4.0 * jnp.tanh(pol_hidden.astype(jnp.float32) * 0.25)
+        pol_exp = jnp.exp(pol_vals)
+        for k, value in enumerate((jnp.exp(ref_vals), pol_exp, pol_exp * (pol_vals - ref_vals))):
+            sums[k, :, columns] += value.reshape(-1, 8, rows).sum(axis=0)
+
+
+def kernel_shards(
+    tokens, gate_weight_base, up_weight_base, adapter_down_stack, adapter_up_stack,
+    segment_block_counts, segment_adapter_ids, segment_live_rows,
+):
+    dp_count = lax.axis_size("dp")
+    tp_count = lax.axis_size("tensor")
+    group_count = lax.axis_size("groups")
+    dp_index = lax.axis_index("dp")
+    tp_index = lax.axis_index("tensor")
+    local_rows, features = tokens.shape
+    units = gate_weight_base.shape[0]
+    ranks = adapter_up_stack.shape[1]
+    total_rows = local_rows * dp_count
+    per_core = dp_count // tp_count
+    rows_half = total_rows // tp_count
+    member, live_rows, counts = segment_tables(segment_block_counts, segment_live_rows, total_rows)
+    row_adapter = jnp.sum(member.astype(jnp.int32) * segment_adapter_ids[:, None], axis=0)
+    f32, bf16 = jnp.float32, jnp.bfloat16
+    any_spec = pl.BlockSpec(memory_space=pl.ANY)
+    dma = pltpu.SemaphoreType.DMA
+    own, peer, adapters, contrib = pl.pallas_call(
+        functools.partial(gather_project, dp_count, tp_count, group_count, units // 2),
+        out_shape=(
+            jax.ShapeDtypeStruct((per_core, 2, units, local_rows), f32),
+            jax.ShapeDtypeStruct((per_core, 2, units, local_rows), f32),
+            jax.ShapeDtypeStruct((dp_count, tp_count * ranks, units), bf16),
+            jax.ShapeDtypeStruct((total_rows, tp_count * ranks), f32),
+        ),
+        in_specs=[any_spec] * 5,
+        out_specs=(any_spec,) * 4,
+        scratch_shapes=[
+            pltpu.VMEM((total_rows, features), bf16),
+            pltpu.VMEM((2, units, features), bf16),
+            pltpu.VMEM((features, tp_count * ranks), bf16),
+            pltpu.VMEM((dp_count, 2, units, local_rows), f32),
+            pltpu.VMEM((total_rows, tp_count * ranks), f32),
+            dma((5,)), dma((dp_count,)), dma((dp_count,)), dma((dp_count,)), dma((dp_count,)),
+            dma((2,)), dma((2,)), dma((dp_count,)), dma((per_core,)), dma((dp_count,)),
+        ],
+        compiler_params=pltpu.CompilerParams(
+            collective_id=0, has_side_effects=True, vmem_limit_bytes=60 * 1024 * 1024
+        ),
+        name="gather_project",
+    )(tokens, gate_weight_base, up_weight_base, adapter_down_stack[0], adapter_up_stack[0])
+    masked = jnp.where((row_adapter == dp_index)[:, None], contrib, 0.0)
+    down_proj = lax.psum(masked, ("dp", "tensor")).astype(bf16)
+    own_down = lax.dynamic_slice_in_dim(down_proj, tp_index * rows_half, rows_half, 0)
+    own_ids = lax.dynamic_slice_in_dim(row_adapter[::local_rows], tp_index * per_core, per_core, 0)
+    chunk = 256
+    ref_hidden, pol_hidden, sums = pl.pallas_call(
+        finish,
+        out_shape=(
+            jax.ShapeDtypeStruct((units, rows_half), bf16),
+            jax.ShapeDtypeStruct((units, rows_half), bf16),
+            jax.ShapeDtypeStruct((3, 8, rows_half), f32),
+        ),
+        grid_spec=pltpu.PrefetchScalarGridSpec(
+            num_scalar_prefetch=1,
+            grid=(units // chunk,),
+            in_specs=[
+                pl.BlockSpec((per_core, 2, chunk, local_rows), lambda u, ids: (0, 0, u, 0)),
+                pl.BlockSpec((per_core, 2, chunk, local_rows), lambda u, ids: (0, 0, u, 0)),
+                pl.BlockSpec((dp_count, tp_count * ranks, chunk), lambda u, ids: (0, 0, u)),
+                pl.BlockSpec((rows_half, tp_count * ranks), lambda u, ids: (0, 0)),
+            ],
+            out_specs=[
+                pl.BlockSpec((chunk, rows_half), lambda u, ids: (u, 0)),
+                pl.BlockSpec((chunk, rows_half), lambda u, ids: (u, 0)),
+                pl.BlockSpec((3, 8, rows_half), lambda u, ids: (0, 0, 0)),
+            ],
+        ),
+        compiler_params=pltpu.CompilerParams(vmem_limit_bytes=40 * 1024 * 1024),
+        name="finish",
+    )(own_ids, own, peer, adapters, own_down)
+    placed = lax.dynamic_update_slice_in_dim(
+        jnp.zeros((3, total_rows), f32), sums.sum(axis=1), tp_index * rows_half, 1
+    )
+    ref_sum, pol_sum, cross_sum = lax.psum(placed, ("dp", "tensor"))
+    kl_row = cross_sum / pol_sum - jnp.log(pol_sum) + jnp.log(ref_sum)
+    seg_kl = jnp.sum(live_rows.astype(f32) * kl_row[None, :], axis=1) / counts
+    return (ref_hidden, pol_hidden, seg_kl)
+
+
+def pick_shards(*args):
+    rows = args[0].shape[0]
+    units = args[1].shape[0]
+    sizes = (lax.axis_size("groups"), lax.axis_size("tensor"))
+    fits = rows == BLOCK and units % 256 == 0 and sizes == (2, 2) and lax.axis_size("dp") % 4 == 0
+    return kernel_shards(*args) if fits else shards(*args)
+
+
 def solution(mesh):
     in_specs = (
         P(("groups", "dp"), "tensor"),
@@ -155,4 +481,4 @@
         P("groups"),
     )
     out_specs = (P("dp", ("groups", "tensor")), P("dp", ("groups", "tensor")), P("groups"))
-    return jax.shard_map(shards, mesh=mesh, in_specs=in_specs, out_specs=out_specs, check_vma=False)
+    return jax.shard_map(pick_shards, mesh=mesh, in_specs=in_specs, out_specs=out_specs, check_vma=False)

time: 788 us -> 261 us (0.33)
  waiting for transfers between devices: 358 us -> 0 us
  Pallas kernels: 0 us -> 130 us
  other arithmetic: 131 us -> 4.26 us
  matrix products: 56.4 us -> 0 us
  blocking collectives: 171 us -> 121 us
  local copies, waits for them, and re-layouts: 48 us -> 5.33 us
  between operations: 15.3 us -> 0.71 us
    psum x4 -> x0, waiting for transfers between devices: 320 us -> none  [spread_2(): return lax.psum(jnp.where(mine, value, jnp.zeros_like(value)), axis)]
    pallas_call x0 -> x2, Pallas kernels: none -> 130 us  [the longest x1 119 us: kernel_shards(): pl.pallas_call(functools.partial(gather_project, dp_count, tp_count, grou...]
    unnamed x2 -> x0, other arithmetic: 79.7 us -> none
    dot_general x8 -> x0, matrix products: 56.4 us -> none  [the longest x1 21.9 us: project_tokens(): lax.dot_general(gate_weight_base, block_rows, contract, preferred_element...]
    psum x2, blocking collectives: 171 us -> 121 us  [the longest x1 63.2 us: kernel_shards(): down_proj = lax.psum(masked, ('dp', 'tensor')).astype(bf16)]
    reduce_scatter x1 -> x0, waiting for transfers between devices: 37.5 us -> none  [shards(): lax.psum_scatter(jnp.stack([base_terms, policy_terms]), 'tensor', scatter...]
    another operation x3 -> x1, other arithmetic: 24.9 us -> 0.83 us  [the longest x2 24 us: shards(): jnp.stack([base_terms, policy_terms])]
    unnamed x13 -> x4, local copies, waits for them, and re-layouts: 28.2 us -> 5.13 us
  transfers between devices with their start and end apart: 7 -> 0, of which waited for: 5 -> 0; matrix products, arithmetic and copies ran while one was open for 16% -> 0% of each run, Pallas kernels for 0% -> 0%
where the time goes in v1:
time: 261 us
  Pallas kernels  130 us (50%)
  blocking collectives  121 us (46%)
  local copies, waits for them, and re-layouts  5.33 us (2%)
  other arithmetic  4.26 us (2%)
    pallas_call x1, Pallas kernels, kernel_shards(): pl.pallas_call(functools.partial(gather_project, dp_count, tp_count, grou...  119 us
    psum x1, blocking collectives, kernel_shards(): down_proj = lax.psum(masked, ('dp', 'tensor')).astype(bf16)  63.2 us
    psum x1, blocking collectives, kernel_shards(): ref_sum, pol_sum, cross_sum = lax.psum(placed, ('dp', 'tensor'))  57.6 us
    pallas_call x1, Pallas kernels, kernel_shards(): pl.pallas_call(finish, out_shape=(jax.ShapeDtypeStruct((units, rows_half)...  10.3 us

profile of v1, /device:TPU:0, one launch (start us, length us, event | category | flops | bytes accessed | tf_op | source)
XLA Modules:
  0.0 260.9 jit_solution(4960770870601396265)
XLA Ops:
  0.6 0.8 reduce-window.8
  1.5 0.7 multiply_add_fusion
  2.1 0.7 select_reduce_fusion.1
  2.9 119.5 %gather_project.1 = (f32[4,2,1792,128]{3,2,1,0:T(8,128)}, f32[4,2,1792,128]{3,2,1,0:T(8,128)}, bf16[8,128,1792]{2,1,0:T(8,128)(2,1)}, f32[1024,128]{1,0:T(8,128)}) custom-call(bf16[128,4096]{1,0:T(8,128)(2,1)} %tokens.1, bf16[1792,4096]{1,0:T(8,128)(2,1)} %gate.1, bf16[1792,4096]{1,0:T(8,128)(2,1)} %up.1, bf16[4096,128]{1,0:T(8,128)(2,1)} %bitcast.8, ...), custom_call_target="tpu_custom_call" | custom-call | tf_op jit(solution)/shard_map/gather_project/pallas_call | solution.py:401
  122.4 1.2 broadcast_select_fusion
  123.7 63.2 %all-reduce.1 = bf16[1024,128]{1,0:T(8,128)(2,1)S(1)} all-reduce(f32[1024,128]{1,0:T(8,128)S(1)} %broadcast_select_fusion), channel_id=1, replica_groups=mesh['groups'=2,'dp'=8,'tensor'=2] {'dp','tensor'}, use_global_device_ids=true, to_apply=%region_2.3 | all-reduce | flops 131072 | bytes 786432 | tf_op jit(solution)/shard_map/psum | solution.py:426
  186.9 0.1 slice.3
  187.0 0.1 dynamic_slice.6.ids
  187.1 0.0 copy-start
  187.1 3.1 %copy-done = f32[4,2,1792,128]{3,2,1,0:T(8,128)S(1)} copy-done((f32[4,2,1792,128]{3,2,1,0:T(8,128)S(1)}, f32[4,2,1792,128]{3,2,1,0:T(8,128)}, u32[]{:S(2)}) %copy-start) | copy-done | bytes 7340056
  190.2 0.0 copy-start.1
  190.2 2.0 copy-done.1
  192.2 10.3 %finish.1 = (bf16[1792,512]{1,0:T(8,128)(2,1)}, bf16[1792,512]{1,0:T(8,128)(2,1)}, f32[3,8,512]{2,1,0:T(8,128)S(1)}) custom-call(s32[4]{0:T(128)S(1)} %dynamic_slice.6.ids, f32[4,2,1792,128]{3,2,1,0:T(8,128)S(1)} %copy-done, f32[4,2,1792,128]{3,2,1,0:T(8,128)} %get-tuple-element.11.peer, bf16[8,128,1792]{2,1,0:T(8,128)(2,1)S(1)} %copy-done.1, ...), custom_call_target="tpu_custom_call" | custom-call | tf_op jit(solution)/shard_map/finish/pallas_call | solution.py:430
  202.5 57.6 %psum.15 = f32[3,1024]{1,0:T(4,128)S(1)} all-reduce(f32[3,1024]{1,0:T(4,128)S(1)} %constant_dynamic-update-slice_fusion), channel_id=1, replica_groups=mesh['groups'=2,'dp'=8,'tensor'=2] {'dp','tensor'}, use_global_device_ids=true, to_apply=%region_4.5 | all-reduce | flops 3072 | bytes 24576 | tf_op jit(solution)/shard_map/psum | solution.py:458
  260.2 0.2 select_reduce_fusion
  260.4 0.5 convert_divide_fusion
  (7 shorter events, 0.1 us)
Async XLA Ops:
  187.1 3.1 %copy-start = (f32[4,2,1792,128]{3,2,1,0:T(8,128)S(1)}, f32[4,2,1792,128]{3,2,1,0:T(8,128)}, u32[]{:S(2)}) copy-start(f32[4,2,1792,128]{3,2,1,0:T(8,128)} %get-tuple-element.10.own) | copy-start | bytes 22020100
  190.2 2.0 copy-start.1

commit v2 on v1

--- a/solution.py
+++ b/solution.py
@@ -161,11 +161,11 @@
 
 def gather_project(
     dp_count, tp_count, group_count, unit_chunk,
-    tokens, gate, up, down, adapter_up,
-    own_out, peer_out, adapters_out, contrib_out,
-    tok_buf, weights, down_buf, parts, contrib,
+    tokens, gate, up, down, adapter_up, owned,
+    own_out, peer_out, adapters_out, down_out,
+    tok_buf, weights, down_buf, parts, contrib, contrib_peer, published, heard,
     load_sem, ring_send, ring_recv, ad_send, ad_recv, pass_send, pass_recv,
-    part_send, part_recv, out_sem,
+    part_send, part_recv, con_send, con_recv, pub_send, pub_recv,
 ):
     half = dp_count // 2
     rows = tokens.shape[0]
@@ -243,11 +243,17 @@
                 parts[slot + b, which, pl.ds(first, unit_chunk), :] = value[:, b * rows:(b + 1) * rows]
             return carry
 
+        lax.fori_loop(0, 2 * (units // unit_chunk), chunk, 0)
+
+    def project_down(slot, blocks):
         contrib[pl.ds(slot * rows, blocks * rows), :] = jnp.dot(
             tok_buf[pl.ds(slot * rows, blocks * rows), :], down_buf[...],
             preferred_element_type=jnp.float32,
         )
-        lax.fori_loop(0, 2 * (units // unit_chunk), chunk, 0)
+        for j in range(slot, slot + blocks):
+            @pl.when(slot_block[j] // per_core != core)
+            def _():
+                contrib_copy(j).start()
 
     per_core = dp_count // tp_count
     slot_place = [place]
@@ -269,14 +275,32 @@
         return pltpu.make_async_copy(parts.at[slot], own_out.at[where], part_send.at[slot])
 
     def contrib_copy(slot):
-        first = pl.multiple_of(slot_block[slot] * rows, rows)
-        return pltpu.make_async_copy(
-            contrib.at[pl.ds(slot * rows, rows)], contrib_out.at[pl.ds(first, rows)], out_sem.at[slot]
-        )
+        where = slot_block[slot] % per_core
+        return pltpu.make_async_remote_copy(
+            src_ref=contrib.at[pl.ds(slot * rows, rows)], dst_ref=contrib_peer.at[where],
+            send_sem=con_send.at[slot], recv_sem=con_recv.at[where],
+            device_id={"tensor": other_core}, device_id_type=MESH,
+        )
+
+    def publish_copy(where, k):
+        return pltpu.make_async_remote_copy(
+            src_ref=published.at[where], dst_ref=heard.at[k - 1, where],
+            send_sem=pub_send.at[k - 1, where], recv_sem=pub_recv.at[k - 1, where],
+            device_id={"dp": (me + k) % dp_count}, device_id_type=MESH,
+        )
+
+    def publish(slot):
+        where = slot_block[slot] % per_core
+
+        @pl.when(slot_block[slot] // per_core == core)
+        def _():
+            contrib_copy(slot).wait_recv()
+            total = contrib[pl.ds(slot * rows, rows), :] + contrib_peer[where]
+            published[where] = (total * owned[slot_block[slot], 0:1, :]).astype(published.dtype)
+            for k in range(1, dp_count):
+                publish_copy(where, k).start()
 
     def hand_over(slot):
-        contrib_copy(slot).start()
-
         @pl.when(slot_block[slot] // per_core == core)
         def _():
             own_copy(slot).start()
@@ -285,8 +309,10 @@
         def _():
             part_copy(slot).start()
 
+    project_down(0, 1)
     project(0, 1)
     hand_over(0)
+    publish(0)
     sent = [cw, ccw]
     passes = []
     for s in range(1, half):
@@ -303,9 +329,12 @@
             ccw = send(tok_buf.at[pl.ds(b, cut)], tok_buf.at[pl.ds(z + cut, cut)],
                        2 * s + 1, "dp", left, ring_send, ring_recv)
         sent += [cw, ccw]
+        project_down(2 * s - 1, 2)
         project(2 * s - 1, 2)
         hand_over(2 * s - 1)
         hand_over(2 * s)
+        publish(2 * s - 1)
+        publish(2 * s)
         if s == half - 2:
             for copy in ad_copies:
                 copy.wait_recv()
@@ -318,15 +347,22 @@
             passes.append(send(region, region, 1, "tensor", other_core, pass_send, pass_recv))
     cw.wait_recv()
     ccw.wait_recv()
+    project_down(last, 1)
+    publish(last)
     project(last, 1)
     hand_over(last)
+    for where in range(per_core):
+        for k in range(1, dp_count):
+            publish_copy(where, k).wait_recv()
+        total = published[where].astype(jnp.float32)
+        for k in range(1, dp_count):
+            total = total + heard[k - 1, where].astype(jnp.float32)
+        down_out[pl.ds(where * rows, rows), :] = total.astype(down_out.dtype)
 
     for copy in sent + ad_copies + passes:
         copy.wait_send()
     passes[1].wait_recv()
     for slot in range(dp_count):
-        contrib_copy(slot).wait()
-
         @pl.when(slot_block[slot] // per_core == core)
         def _():
             own_copy(slot).wait()
@@ -334,8 +370,11 @@
         @pl.when(slot_block[slot] // per_core != core)
         def _():
             part_copy(slot).wait_send()
+            contrib_copy(slot).wait_send()
 
     for where in range(per_core):
+        for k in range(1, dp_count):
+            publish_copy(where, k).wait_send()
         pltpu.make_async_remote_copy(
             src_ref=parts.at[where], dst_ref=peer_out.at[where],
             send_sem=part_send.at[where], recv_sem=part_recv.at[where],
@@ -376,6 +415,45 @@
         pol_exp = jnp.exp(pol_vals)
         for k, value in enumerate((jnp.exp(ref_vals), pol_exp, pol_exp * (pol_vals - ref_vals))):
             sums[k, :, columns] += value.reshape(-1, 8, rows).sum(axis=0)
+
+
+def divergence(dp_count, sums, live, out, mine, heard, halves, send_sem, recv_sem):
+    me = lax.axis_index("dp")
+    other_core = 1 - lax.axis_index("tensor")
+    barrier = pltpu.get_barrier_semaphore()
+    for k in range(1, dp_count):
+        pl.semaphore_signal(barrier, inc=1, device_id={"dp": (me + k) % dp_count}, device_id_type=MESH)
+    pl.semaphore_signal(barrier, inc=1, device_id={"tensor": other_core}, device_id_type=MESH)
+    for k in range(3):
+        mine[k:k + 1, :] = jnp.sum(sums[k], axis=0, keepdims=True)
+    mine[3:8, :] = jnp.zeros((5, mine.shape[1]), jnp.float32)
+    pl.semaphore_wait(barrier, dp_count)
+    copies = []
+    for k in range(1, dp_count):
+        copies.append(pltpu.make_async_remote_copy(
+            src_ref=mine, dst_ref=heard.at[me], send_sem=send_sem.at[k], recv_sem=recv_sem.at[k],
+            device_id={"dp": (me + k) % dp_count}, device_id_type=MESH,
+        ))
+        copies[-1].start()
+    for copy in copies:
+        copy.wait_recv()
+    heard[me] = mine[...]
+    total = heard[0]
+    for k in range(1, dp_count):
+        total = total + heard[k]
+    ref_sum, pol_sum, cross_sum = total[0:1], total[1:2], total[2:3]
+    kl_row = cross_sum / pol_sum - jnp.log(pol_sum) + jnp.log(ref_sum)
+    part = jnp.sum(live[...] * kl_row, axis=1, keepdims=True)
+    halves[0] = jnp.broadcast_to(part, (8, 128))
+    swap = pltpu.make_async_remote_copy(
+        src_ref=halves.at[0], dst_ref=halves.at[1], send_sem=send_sem.at[0], recv_sem=recv_sem.at[0],
+        device_id={"tensor": other_core}, device_id_type=MESH,
+    )
+    swap.start()
+    swap.wait()
+    for copy in copies:
+        copy.wait_send()
+    out[...] = halves[0] + halves[1]
 
 
 def kernel_shards(
@@ -398,33 +476,39 @@
     f32, bf16 = jnp.float32, jnp.bfloat16
     any_spec = pl.BlockSpec(memory_space=pl.ANY)
     dma = pltpu.SemaphoreType.DMA
-    own, peer, adapters, contrib = pl.pallas_call(
+    owned = jnp.broadcast_to(
+        (row_adapter[::local_rows] == dp_index).astype(f32)[:, None, None],
+        (dp_count, 8, tp_count * ranks),
+    )
+    vmem_spec = pl.BlockSpec(memory_space=pltpu.VMEM)
+    own, peer, adapters, own_down = pl.pallas_call(
         functools.partial(gather_project, dp_count, tp_count, group_count, units // 2),
         out_shape=(
             jax.ShapeDtypeStruct((per_core, 2, units, local_rows), f32),
             jax.ShapeDtypeStruct((per_core, 2, units, local_rows), f32),
             jax.ShapeDtypeStruct((dp_count, tp_count * ranks, units), bf16),
-            jax.ShapeDtypeStruct((total_rows, tp_count * ranks), f32),
+            jax.ShapeDtypeStruct((rows_half, tp_count * ranks), bf16),
         ),
-        in_specs=[any_spec] * 5,
-        out_specs=(any_spec,) * 4,
+        in_specs=[any_spec] * 5 + [vmem_spec],
+        out_specs=(any_spec,) * 3 + (vmem_spec,),
         scratch_shapes=[
             pltpu.VMEM((total_rows, features), bf16),
             pltpu.VMEM((2, units, features), bf16),
             pltpu.VMEM((features, tp_count * ranks), bf16),
             pltpu.VMEM((dp_count, 2, units, local_rows), f32),
             pltpu.VMEM((total_rows, tp_count * ranks), f32),
+            pltpu.VMEM((per_core, local_rows, tp_count * ranks), f32),
+            pltpu.VMEM((per_core, local_rows, tp_count * ranks), bf16),
+            pltpu.VMEM((dp_count - 1, per_core, local_rows, tp_count * ranks), bf16),
             dma((5,)), dma((dp_count,)), dma((dp_count,)), dma((dp_count,)), dma((dp_count,)),
-            dma((2,)), dma((2,)), dma((dp_count,)), dma((per_core,)), dma((dp_count,)),
+            dma((2,)), dma((2,)), dma((dp_count,)), dma((per_core,)), dma((dp_count,)), dma((per_core,)),
+            dma((dp_count - 1, per_core)), dma((dp_count - 1, per_core)),
         ],
         compiler_params=pltpu.CompilerParams(
             collective_id=0, has_side_effects=True, vmem_limit_bytes=60 * 1024 * 1024
         ),
         name="gather_project",
-    )(tokens, gate_weight_base, up_weight_base, adapter_down_stack[0], adapter_up_stack[0])
-    masked = jnp.where((row_adapter == dp_index)[:, None], contrib, 0.0)
-    down_proj = lax.psum(masked, ("dp", "tensor")).astype(bf16)
-    own_down = lax.dynamic_slice_in_dim(down_proj, tp_index * rows_half, rows_half, 0)
+    )(tokens, gate_weight_base, up_weight_base, adapter_down_stack[0], adapter_up_stack[0], owned)
     own_ids = lax.dynamic_slice_in_dim(row_adapter[::local_rows], tp_index * per_core, per_core, 0)
     chunk = 256
     ref_hidden, pol_hidden, sums = pl.pallas_call(
@@ -449,15 +533,27 @@
                 pl.BlockSpec((3, 8, rows_half), lambda u, ids: (0, 0, 0)),
             ],
         ),
-        compiler_params=pltpu.CompilerParams(vmem_limit_bytes=40 * 1024 * 1024),
+        compiler_params=pltpu.CompilerParams(vmem_limit_bytes=60 * 1024 * 1024),
         name="finish",
     )(own_ids, own, peer, adapters, own_down)
-    placed = lax.dynamic_update_slice_in_dim(
-        jnp.zeros((3, total_rows), f32), sums.sum(axis=1), tp_index * rows_half, 1
-    )
-    ref_sum, pol_sum, cross_sum = lax.psum(placed, ("dp", "tensor"))
-    kl_row = cross_sum / pol_sum - jnp.log(pol_sum) + jnp.log(ref_sum)
-    seg_kl = jnp.sum(live_rows.astype(f32) * kl_row[None, :], axis=1) / counts
+    seg_count = live_rows.shape[0]
+    spread = jnp.zeros((8, total_rows), f32).at[:seg_count].set(live_rows.astype(f32))
+    own_live = lax.dynamic_slice_in_dim(spread, tp_index * rows_half, rows_half, 1)
+    seg_sums = pl.pallas_call(
+        functools.partial(divergence, dp_count),
+        out_shape=jax.ShapeDtypeStruct((8, 128), f32),
+        in_specs=[vmem_spec] * 2,
+        out_specs=vmem_spec,
+        scratch_shapes=[
+            pltpu.VMEM((8, rows_half), f32),
+            pltpu.VMEM((dp_count, 8, rows_half), f32),
+            pltpu.VMEM((2, 8, 128), f32),
+            dma((dp_count,)), dma((dp_count,)),
+        ],
+        compiler_params=pltpu.CompilerParams(collective_id=1, has_side_effects=True),
+        name="divergence",
+    )(sums, own_live)
+    seg_kl = seg_sums[:seg_count, 0] / counts
     return (ref_hidden, pol_hidden, seg_kl)
 
 

time: 261 us -> 166 us (0.64)
  blocking collectives: 121 us -> 0 us
  Pallas kernels: 130 us -> 159 us
  local copies, waits for them, and re-layouts: 5.33 us -> 2.16 us
    psum x2 -> x0, blocking collectives: 121 us -> none  [the longest x1 63.2 us: kernel_shards(): down_proj = lax.psum(masked, ('dp', 'tensor')).astype(bf16)]
    pallas_call x1, Pallas kernels: 119 us -> 135 us  [kernel_shards(): pl.pallas_call(functools.partial(gather_project, dp_count, tp_count, grou...]
    pallas_call x0 -> x1, Pallas kernels: none -> 12.4 us  [kernel_shards(): pl.pallas_call(functools.partial(divergence, dp_count), out_shape=jax.Sha...]
    unnamed x4 -> x0, local copies, waits for them, and re-layouts: 5.13 us -> none
where the time goes in v2:
time: 166 us
  Pallas kernels  159 us (96%)
  other arithmetic  3.46 us (2%)
  local copies, waits for them, and re-layouts  2.16 us (1%)
    pallas_call x1, Pallas kernels, kernel_shards(): pl.pallas_call(functools.partial(gather_project, dp_count, tp_count, grou...  135 us
    pallas_call x1, Pallas kernels, kernel_shards(): pl.pallas_call(finish, out_shape=(jax.ShapeDtypeStruct((units, rows_half)...  12.4 us
    pallas_call x1, Pallas kernels, kernel_shards(): pl.pallas_call(functools.partial(divergence, dp_count), out_shape=jax.Sha...  12.4 us

profile of v2, /device:TPU:0, one launch (start us, length us, event | category | flops | bytes accessed | tf_op | source)
XLA Modules:
  0.0 165.7 jit_solution(9230706728741836207)
XLA Ops:
  0.6 0.8 reduce-window.8
  1.5 0.7 multiply_add_fusion
  2.1 0.7 select_reduce_fusion
  2.9 0.1 slice.23
  3.0 0.6 dynamic_slice.6.ids
  3.6 0.7 broadcast_in_dim.2.owned
  4.3 134.5 %gather_project.1 = (f32[4,2,1792,128]{3,2,1,0:T(8,128)}, f32[4,2,1792,128]{3,2,1,0:T(8,128)}, bf16[8,128,1792]{2,1,0:T(8,128)(2,1)}, bf16[512,128]{1,0:T(8,128)(2,1)}) custom-call(bf16[128,4096]{1,0:T(8,128)(2,1)} %tokens.1, bf16[1792,4096]{1,0:T(8,128)(2,1)} %gate.1, bf16[1792,4096]{1,0:T(8,128)(2,1)} %up.1, bf16[4096,128]{1,0:T(8,128)(2,1)} %bitcast.7, ...), custom_call_target="tpu_custom_call" | custom-call | tf_op jit(solution)/shard_map/gather_project/pallas_call | solution.py:484
  138.8 12.4 %finish.1 = (bf16[1792,512]{1,0:T(8,128)(2,1)}, bf16[1792,512]{1,0:T(8,128)(2,1)}, f32[3,8,512]{2,1,0:T(8,128)}) custom-call(s32[4]{0:T(128)} %dynamic_slice.6.ids, f32[4,2,1792,128]{3,2,1,0:T(8,128)} %get-tuple-element.22.own, f32[4,2,1792,128]{3,2,1,0:T(8,128)} %get-tuple-element.23.peer, bf16[8,128,1792]{2,1,0:T(8,128)(2,1)} %get-tuple-element.24.adapters, ...), custom_call_target="tpu_custom_call" | custom-call | tf_op jit(solution)/shard_map/finish/pallas_call | solution.py:514
  151.3 0.1 fusion
  151.4 0.6 fusion.1.live
  152.0 12.4 %divergence.1 = f32[8,128]{1,0:T(8,128)} custom-call(f32[3,8,512]{2,1,0:T(8,128)} %get-tuple-element.28.sums, f32[8,512]{1,0:T(8,128)} %fusion.1.live), custom_call_target="tpu_custom_call" | custom-call | tf_op jit(solution)/shard_map/divergence/pallas_call | solution.py:542
  164.3 0.8 slice_reduce_fusion
  165.1 0.5 convert_divide_fusion
  (2 shorter events, 0.0 us)

commit v3 on v2

--- a/solution.py
+++ b/solution.py
@@ -15,7 +15,9 @@
 
 
 def segment_tables(segment_block_counts, segment_live_rows, total_rows):
-    seg_ends = jnp.cumsum(segment_block_counts)
+    order = jnp.arange(segment_block_counts.shape[0])
+    before = order[None, :] <= order[:, None]
+    seg_ends = jnp.sum(jnp.where(before, segment_block_counts[None, :], 0), axis=1)
     starts = seg_ends - segment_block_counts
     row_ids = jnp.arange(total_rows, dtype=jnp.int32)
     blocks = row_ids // BLOCK
@@ -163,9 +165,10 @@
     dp_count, tp_count, group_count, unit_chunk,
     tokens, gate, up, down, adapter_up, owned,
     own_out, peer_out, adapters_out, down_out,
-    tok_buf, weights, down_buf, parts, contrib, contrib_peer, published, heard,
+    tok_buf, weights, down_buf, parts, contrib, contrib_peer, published, heard, reduced, gathered,
     load_sem, ring_send, ring_recv, ad_send, ad_recv, pass_send, pass_recv,
     part_send, part_recv, con_send, con_recv, pub_send, pub_recv,
+    red_send, red_recv,
 ):
     half = dp_count // 2
     rows = tokens.shape[0]
@@ -230,7 +233,7 @@
     for load in loads:
         load.wait()
 
-    def project(slot, blocks):
+    def project(slot, blocks, matrices=(0, 2)):
         def chunk(step, carry):
             which = step // (units // unit_chunk)
             first = pl.multiple_of((step % (units // unit_chunk)) * unit_chunk, unit_chunk)
@@ -243,7 +246,8 @@
                 parts[slot + b, which, pl.ds(first, unit_chunk), :] = value[:, b * rows:(b + 1) * rows]
             return carry
 
-        lax.fori_loop(0, 2 * (units // unit_chunk), chunk, 0)
+        per_matrix = units // unit_chunk
+        lax.fori_loop(matrices[0] * per_matrix, matrices[1] * per_matrix, chunk, 0)
 
     def project_down(slot, blocks):
         contrib[pl.ds(slot * rows, blocks * rows), :] = jnp.dot(
@@ -282,9 +286,13 @@
             device_id={"tensor": other_core}, device_id_type=MESH,
         )
 
+    strip = rows // dp_count
+
     def publish_copy(where, k):
+        target = (me + k) % dp_count
         return pltpu.make_async_remote_copy(
-            src_ref=published.at[where], dst_ref=heard.at[k - 1, where],
+            src_ref=published.at[where, pl.ds(pl.multiple_of(target * strip, 16), strip)],
+            dst_ref=heard.at[k - 1, where],
             send_sem=pub_send.at[k - 1, where], recv_sem=pub_recv.at[k - 1, where],
             device_id={"dp": (me + k) % dp_count}, device_id_type=MESH,
         )
@@ -349,17 +357,29 @@
     ccw.wait_recv()
     project_down(last, 1)
     publish(last)
-    project(last, 1)
-    hand_over(last)
+    project(last, 1, (0, 1))
     for where in range(per_core):
         for k in range(1, dp_count):
             publish_copy(where, k).wait_recv()
-        total = published[where].astype(jnp.float32)
+        total = published[where, pl.ds(pl.multiple_of(me * strip, 16), strip), :].astype(jnp.float32)
         for k in range(1, dp_count):
             total = total + heard[k - 1, where].astype(jnp.float32)
-        down_out[pl.ds(where * rows, rows), :] = total.astype(down_out.dtype)
-
-    for copy in sent + ad_copies + passes:
+        reduced[where] = total.astype(reduced.dtype)
+    spreads = []
+    for k in range(1, dp_count):
+        spreads.append(send(
+            reduced, gathered.at[me], k, "dp", (me + k) % dp_count, red_send, red_recv
+        ))
+    project(last, 1, (1, 2))
+    hand_over(last)
+    for copy in spreads:
+        copy.wait_recv()
+    gathered[me] = reduced[...]
+    for where in range(per_core):
+        for d in range(dp_count):
+            down_out[pl.ds(where * rows + d * strip, strip), :] = gathered[d, where]
+
+    for copy in sent + ad_copies + passes + spreads:
         copy.wait_send()
     passes[1].wait_recv()
     for slot in range(dp_count):
@@ -499,10 +519,12 @@
             pltpu.VMEM((total_rows, tp_count * ranks), f32),
             pltpu.VMEM((per_core, local_rows, tp_count * ranks), f32),
             pltpu.VMEM((per_core, local_rows, tp_count * ranks), bf16),
-            pltpu.VMEM((dp_count - 1, per_core, local_rows, tp_count * ranks), bf16),
+            pltpu.VMEM((dp_count - 1, per_core, local_rows // dp_count, tp_count * ranks), bf16),
+            pltpu.VMEM((per_core, local_rows // dp_count, tp_count * ranks), bf16),
+            pltpu.VMEM((dp_count, per_core, local_rows // dp_count, tp_count * ranks), bf16),
             dma((5,)), dma((dp_count,)), dma((dp_count,)), dma((dp_count,)), dma((dp_count,)),
             dma((2,)), dma((2,)), dma((dp_count,)), dma((per_core,)), dma((dp_count,)), dma((per_core,)),
-            dma((dp_count - 1, per_core)), dma((dp_count - 1, per_core)),
+            dma((dp_count - 1, per_core)), dma((dp_count - 1, per_core)), dma((dp_count,)), dma((dp_count,)),
         ],
         compiler_params=pltpu.CompilerParams(
             collective_id=0, has_side_effects=True, vmem_limit_bytes=60 * 1024 * 1024
@@ -561,7 +583,7 @@
     rows = args[0].shape[0]
     units = args[1].shape[0]
     sizes = (lax.axis_size("groups"), lax.axis_size("tensor"))
-    fits = rows == BLOCK and units % 256 == 0 and sizes == (2, 2) and lax.axis_size("dp") % 4 == 0
+    fits = rows == BLOCK and units % 256 == 0 and sizes == (2, 2) and lax.axis_size("dp") == 8
     return kernel_shards(*args) if fits else shards(*args)
 
 

time: 166 us -> 152 us (0.916)
  Pallas kernels: 159 us -> 146 us
    pallas_call x1, Pallas kernels: 135 us -> 123 us  [kernel_shards(): pl.pallas_call(functools.partial(gather_project, dp_count, tp_count, grou...]
    pallas_call x1, Pallas kernels: 12.4 us -> 10.3 us  [kernel_shards(): pl.pallas_call(functools.partial(divergence, dp_count), out_shape=jax.Sha...]
where the time goes in v3:
time: 152 us
  Pallas kernels  146 us (96%)
  other arithmetic  3.41 us (2%)
  local copies, waits for them, and re-layouts  2.16 us (1%)
    pallas_call x1, Pallas kernels, kernel_shards(): pl.pallas_call(functools.partial(gather_project, dp_count, tp_count, grou...  123 us
    pallas_call x1, Pallas kernels, kernel_shards(): pl.pallas_call(finish, out_shape=(jax.ShapeDtypeStruct((units, rows_half)...  12.4 us
    pallas_call x1, Pallas kernels, kernel_shards(): pl.pallas_call(functools.partial(divergence, dp_count), out_shape=jax.Sha...  10.3 us

profile of v3, /device:TPU:0, one launch (start us, length us, event | category | flops | bytes accessed | tf_op | source)
XLA Modules:
  0.0 152.0 jit_solution(2368087247289208801)
XLA Ops:
  0.6 0.8 select_reduce_fusion.1
  1.4 0.7 multiply_add_fusion
  2.1 0.7 select_reduce_fusion
  2.8 0.1 slice.23
  2.9 0.6 dynamic_slice.6.ids
  3.5 0.7 broadcast_in_dim.16.owned
  4.2 123.0 %gather_project.1 = (f32[4,2,1792,128]{3,2,1,0:T(8,128)}, f32[4,2,1792,128]{3,2,1,0:T(8,128)}, bf16[8,128,1792]{2,1,0:T(8,128)(2,1)}, bf16[512,128]{1,0:T(8,128)(2,1)}) custom-call(bf16[128,4096]{1,0:T(8,128)(2,1)} %tokens.1, bf16[1792,4096]{1,0:T(8,128)(2,1)} %gate.1, bf16[1792,4096]{1,0:T(8,128)(2,1)} %up.1, bf16[4096,128]{1,0:T(8,128)(2,1)} %bitcast.3, ...), custom_call_target="tpu_custom_call" | custom-call | tf_op jit(solution)/shard_map/gather_project/pallas_call | solution.py:504
  127.3 12.4 %finish.1 = (bf16[1792,512]{1,0:T(8,128)(2,1)}, bf16[1792,512]{1,0:T(8,128)(2,1)}, f32[3,8,512]{2,1,0:T(8,128)}) custom-call(s32[4]{0:T(128)} %dynamic_slice.6.ids, f32[4,2,1792,128]{3,2,1,0:T(8,128)} %get-tuple-element.22.own, f32[4,2,1792,128]{3,2,1,0:T(8,128)} %get-tuple-element.23.peer, bf16[8,128,1792]{2,1,0:T(8,128)(2,1)} %get-tuple-element.24.adapters, ...), custom_call_target="tpu_custom_call" | custom-call | tf_op jit(solution)/shard_map/finish/pallas_call | solution.py:536
  139.7 0.1 fusion
  139.8 0.6 fusion.1.live
  140.4 10.3 %divergence.1 = f32[8,128]{1,0:T(8,128)} custom-call(f32[3,8,512]{2,1,0:T(8,128)} %get-tuple-element.28.sums, f32[8,512]{1,0:T(8,128)} %fusion.1.live), custom_call_target="tpu_custom_call" | custom-call | tf_op jit(solution)/shard_map/divergence/pallas_call | solution.py:564
  150.7 0.8 slice_reduce_fusion
  151.5 0.5 convert_divide_fusion
  (2 shorter events, 0.0 us)

commit v4 on v3

--- a/solution.py
+++ b/solution.py
@@ -168,7 +168,7 @@
     tok_buf, weights, down_buf, parts, contrib, contrib_peer, published, heard, reduced, gathered,
     load_sem, ring_send, ring_recv, ad_send, ad_recv, pass_send, pass_recv,
     part_send, part_recv, con_send, con_recv, pub_send, pub_recv,
-    red_send, red_recv,
+    red_send, red_recv, cross_send, cross_recv,
 ):
     half = dp_count // 2
     rows = tokens.shape[0]
@@ -193,13 +193,24 @@
     def block(slot):
         return tok_buf.at[pl.ds(slot * rows, rows)]
 
-    def send(src, dst, sem, axis, target, sends, recvs):
-        copy = pltpu.make_async_remote_copy(
+    def plan(src, dst, sem, axis, target, sends, recvs):
+        return pltpu.make_async_remote_copy(
             src_ref=src, dst_ref=dst, send_sem=sends.at[sem], recv_sem=recvs.at[sem],
             device_id={axis: target}, device_id_type=MESH,
         )
+
+    def send(*where):
+        copy = plan(*where)
         copy.start()
         return copy
+
+    def inside(place_value):
+        return (place_value % half) * (half - 1 - place_value % half) > 0
+
+    across = ring_index(dp_count - 1 - place, dp_count)
+    middle = inside(place)
+    right_end = jnp.logical_not(inside((place + 1) % dp_count))
+    left_end = jnp.logical_not(inside((place + dp_count - 1) % dp_count))
 
     last = dp_count - 1
     cut = rows // 2
@@ -332,11 +343,19 @@
         else:
             a, b = (2 * s - 1) * rows, 2 * s * rows + cut
             z = last * rows
-            cw = send(tok_buf.at[pl.ds(a, cut)], tok_buf.at[pl.ds(z, cut)],
-                      2 * s, "dp", right, ring_send, ring_recv)
-            ccw = send(tok_buf.at[pl.ds(b, cut)], tok_buf.at[pl.ds(z + cut, cut)],
-                       2 * s + 1, "dp", left, ring_send, ring_recv)
-        sent += [cw, ccw]
+            last_cw = plan(tok_buf.at[pl.ds(a, cut)], tok_buf.at[pl.ds(z, cut)],
+                           2 * s, "dp", right, ring_send, ring_recv)
+            last_ccw = plan(tok_buf.at[pl.ds(b, cut)], tok_buf.at[pl.ds(z + cut, cut)],
+                            2 * s + 1, "dp", left, ring_send, ring_recv)
+            pl.when(right_end)(last_cw.start)
+            pl.when(left_end)(last_ccw.start)
+        if s < half - 1:
+            sent += [cw, ccw]
+        if s == 1:
+            source = pl.multiple_of((1 + place % 2) * rows, rows)
+            crossing = plan(tok_buf.at[pl.ds(source, rows)], block(last),
+                            0, "dp", across, cross_send, cross_recv)
+            pl.when(middle)(crossing.start)
         project_down(2 * s - 1, 2)
         project(2 * s - 1, 2)
         hand_over(2 * s - 1)
@@ -353,8 +372,17 @@
             passes[0].wait_recv()
             region = adapters_out.at[:, pl.ds(pl.multiple_of(core * ranks, 16), ranks)]
             passes.append(send(region, region, 1, "tensor", other_core, pass_send, pass_recv))
-    cw.wait_recv()
-    ccw.wait_recv()
+
+    @pl.when(middle)
+    def _():
+        crossing.wait_recv()
+        crossing.wait_send()
+
+    @pl.when(jnp.logical_not(middle))
+    def _():
+        last_cw.wait_recv()
+        last_ccw.wait_recv()
+
     project_down(last, 1)
     publish(last)
     project(last, 1, (0, 1))
@@ -379,6 +407,8 @@
         for d in range(dp_count):
             down_out[pl.ds(where * rows + d * strip, strip), :] = gathered[d, where]
 
+    pl.when(right_end)(last_cw.wait_send)
+    pl.when(left_end)(last_ccw.wait_send)
     for copy in sent + ad_copies + passes + spreads:
         copy.wait_send()
     passes[1].wait_recv()
@@ -525,6 +555,7 @@
             dma((5,)), dma((dp_count,)), dma((dp_count,)), dma((dp_count,)), dma((dp_count,)),
             dma((2,)), dma((2,)), dma((dp_count,)), dma((per_core,)), dma((dp_count,)), dma((per_core,)),
             dma((dp_count - 1, per_core)), dma((dp_count - 1, per_core)), dma((dp_count,)), dma((dp_count,)),
+            dma((1,)), dma((1,)),
         ],
         compiler_params=pltpu.CompilerParams(
             collective_id=0, has_side_effects=True, vmem_limit_bytes=60 * 1024 * 1024

time: 152 us -> 152 us (level)
  no operation moved by 1% of the time
where the time goes in v4:
time: 152 us
  Pallas kernels  146 us (96%)
  other arithmetic  3.41 us (2%)
  local copies, waits for them, and re-layouts  2.16 us (1%)
    pallas_call x1, Pallas kernels, kernel_shards(): pl.pallas_call(functools.partial(gather_project, dp_count, tp_count, grou...  123 us
    pallas_call x1, Pallas kernels, kernel_shards(): pl.pallas_call(finish, out_shape=(jax.ShapeDtypeStruct((units, rows_half)...  12.4 us
    pallas_call x1, Pallas kernels, kernel_shards(): pl.pallas_call(functools.partial(divergence, dp_count), out_shape=jax.Sha...  10.3 us

profile of v4, /device:TPU:0, one launch (start us, length us, event | category | flops | bytes accessed | tf_op | source)
XLA Modules:
  0.0 152.0 jit_solution(262748818466094261)
XLA Ops:
  0.6 0.8 select_reduce_fusion.1
  1.4 0.7 multiply_add_fusion
  2.1 0.7 select_reduce_fusion
  2.8 0.1 slice.23
  2.9 0.6 dynamic_slice.6.ids
  3.5 0.7 broadcast_in_dim.16.owned
  4.2 123.1 %gather_project.1 = (f32[4,2,1792,128]{3,2,1,0:T(8,128)}, f32[4,2,1792,128]{3,2,1,0:T(8,128)}, bf16[8,128,1792]{2,1,0:T(8,128)(2,1)}, bf16[512,128]{1,0:T(8,128)(2,1)}) custom-call(bf16[128,4096]{1,0:T(8,128)(2,1)} %tokens.1, bf16[1792,4096]{1,0:T(8,128)(2,1)} %gate.1, bf16[1792,4096]{1,0:T(8,128)(2,1)} %up.1, bf16[4096,128]{1,0:T(8,128)(2,1)} %bitcast.3, ...), custom_call_target="tpu_custom_call" | custom-call | tf_op jit(solution)/shard_map/gather_project/pallas_call | solution.py:534
  127.3 12.4 %finish.1 = (bf16[1792,512]{1,0:T(8,128)(2,1)}, bf16[1792,512]{1,0:T(8,128)(2,1)}, f32[3,8,512]{2,1,0:T(8,128)}) custom-call(s32[4]{0:T(128)} %dynamic_slice.6.ids, f32[4,2,1792,128]{3,2,1,0:T(8,128)} %get-tuple-element.22.own, f32[4,2,1792,128]{3,2,1,0:T(8,128)} %get-tuple-element.23.peer, bf16[8,128,1792]{2,1,0:T(8,128)(2,1)} %get-tuple-element.24.adapters, ...), custom_call_target="tpu_custom_call" | custom-call | tf_op jit(solution)/shard_map/finish/pallas_call | solution.py:567
  139.7 0.1 fusion
  139.8 0.6 fusion.1.live
  140.4 10.3 %divergence.1 = f32[8,128]{1,0:T(8,128)} custom-call(f32[3,8,512]{2,1,0:T(8,128)} %get-tuple-element.28.sums, f32[8,512]{1,0:T(8,128)} %fusion.1.live), custom_call_target="tpu_custom_call" | custom-call | tf_op jit(solution)/shard_map/divergence/pallas_call | solution.py:595
  150.7 0.8 slice_reduce_fusion
  151.5 0.5 convert_divide_fusion
  (2 shorter events, 0.0 us)

commit v5 on v4

--- a/solution.py
+++ b/solution.py
@@ -336,9 +336,10 @@
     passes = []
     for s in range(1, half):
         cw.wait_recv()
-        ccw.wait_recv()
         if s < half - 1:
+            before = ccw
             cw = send(block(2 * s - 1), block(2 * s + 1), 2 * s, "dp", right, ring_send, ring_recv)
+            before.wait_recv()
             ccw = send(block(2 * s), block(2 * s + 2), 2 * s + 1, "dp", left, ring_send, ring_recv)
         else:
             a, b = (2 * s - 1) * rows, 2 * s * rows + cut
@@ -348,6 +349,7 @@
             last_ccw = plan(tok_buf.at[pl.ds(b, cut)], tok_buf.at[pl.ds(z + cut, cut)],
                             2 * s + 1, "dp", left, ring_send, ring_recv)
             pl.when(right_end)(last_cw.start)
+            ccw.wait_recv()
             pl.when(left_end)(last_ccw.start)
         if s < half - 1:
             sent += [cw, ccw]

time: 152 us -> 154 us (1.013)
  no operation moved by 1% of the time
where the time goes in v5:
time: 154 us; the launch traced here: 153 us
  Pallas kernels  147 us (95%)
  other arithmetic  3.41 us (2%)
  local copies, waits for them, and re-layouts  2.16 us (1%)
    pallas_call x1, Pallas kernels, kernel_shards(): pl.pallas_call(functools.partial(gather_project, dp_count, tp_count, grou...  123 us
    pallas_call x1, Pallas kernels, kernel_shards(): pl.pallas_call(finish, out_shape=(jax.ShapeDtypeStruct((units, rows_half)...  12.4 us
    pallas_call x1, Pallas kernels, kernel_shards(): pl.pallas_call(functools.partial(divergence, dp_count), out_shape=jax.Sha...  11.6 us

profile of v5, /device:TPU:0, one launch (start us, length us, event | category | flops | bytes accessed | tf_op | source)
XLA Modules:
  0.0 153.3 jit_solution(14733719264124923986)
XLA Ops:
  0.6 0.8 select_reduce_fusion.1
  1.4 0.7 multiply_add_fusion
  2.1 0.7 select_reduce_fusion
  2.8 0.1 slice.23
  2.9 0.6 dynamic_slice.6.ids
  3.5 0.7 broadcast_in_dim.16.owned
  4.2 123.0 %gather_project.1 = (f32[4,2,1792,128]{3,2,1,0:T(8,128)}, f32[4,2,1792,128]{3,2,1,0:T(8,128)}, bf16[8,128,1792]{2,1,0:T(8,128)(2,1)}, bf16[512,128]{1,0:T(8,128)(2,1)}) custom-call(bf16[128,4096]{1,0:T(8,128)(2,1)} %tokens.1, bf16[1792,4096]{1,0:T(8,128)(2,1)} %gate.1, bf16[1792,4096]{1,0:T(8,128)(2,1)} %up.1, bf16[4096,128]{1,0:T(8,128)(2,1)} %bitcast.3, ...), custom_call_target="tpu_custom_call" | custom-call | tf_op jit(solution)/shard_map/gather_project/pallas_call | solution.py:536
  127.3 12.4 %finish.1 = (bf16[1792,512]{1,0:T(8,128)(2,1)}, bf16[1792,512]{1,0:T(8,128)(2,1)}, f32[3,8,512]{2,1,0:T(8,128)}) custom-call(s32[4]{0:T(128)} %dynamic_slice.6.ids, f32[4,2,1792,128]{3,2,1,0:T(8,128)} %get-tuple-element.22.own, f32[4,2,1792,128]{3,2,1,0:T(8,128)} %get-tuple-element.23.peer, bf16[8,128,1792]{2,1,0:T(8,128)(2,1)} %get-tuple-element.24.adapters, ...), custom_call_target="tpu_custom_call" | custom-call | tf_op jit(solution)/shard_map/finish/pallas_call | solution.py:569
  139.7 0.1 fusion
  139.8 0.6 fusion.1.live
  140.4 11.6 %divergence.1 = f32[8,128]{1,0:T(8,128)} custom-call(f32[3,8,512]{2,1,0:T(8,128)} %get-tuple-element.28.sums, f32[8,512]{1,0:T(8,128)} %fusion.1.live), custom_call_target="tpu_custom_call" | custom-call | tf_op jit(solution)/shard_map/divergence/pallas_call | solution.py:597
  152.0 0.8 slice_reduce_fusion
  152.8 0.5 convert_divide_fusion
  (2 shorter events, 0.0 us)
